TPU v7x, 128 devices: a whole 4x4x4 slice. The times are simulated.
128 devices in a mesh: section: 2 (over x_lo), dp: 8 (over x_hi, y), tensor: 8 (over z, core).
Axes of the slice: x: 4 (x_hi: 2, x_lo: 2; x = x_hi * 2 + x_lo), y: 4, z: 4, core: 2. Of those that a mesh axis runs over, the one named last changes fastest.
Arguments:
- tokens: bfloat16 [2048, 8192], P('dp', ('section', 'tensor')), may hold values from -6 to 6
- segment_ids: int32 [8, 256], P('dp'), may hold values from 0 to 3, never falling along the last dimension, each value on 1 to 128 neighbouring positions
- gain_attn: float32 [8192], replicated, may hold values from 0.1 to 1.9
- w_query: bfloat16 [8192, 4096], P(None, ('section', 'tensor')), may hold values from -0.06629126 to 0.06629126
- w_key: bfloat16 [8192, 4096], P(None, ('section', 'tensor')), may hold values from -0.06629126 to 0.06629126
- w_value: bfloat16 [8192, 4096], P(None, ('section', 'tensor')), may hold values from -0.0625 to 0.0625
- w_output: bfloat16 [4096, 8192], P(('section', 'tensor')), may hold values from -0.09375 to 0.09375
- gain_ffn: float32 [8192], replicated, may hold values from 0.1 to 1.9
- w_up: bfloat16 [8192, 16384], P(('section', 'tensor'), 'dp'), may hold values from -0.0625 to 0.0625
- w_down: bfloat16 [16384, 8192], P('dp', ('section', 'tensor')), may hold values from -0.046875 to 0.046875
Outputs:
- layer_out: bfloat16 [2048, 8192], P('dp', ('section', 'tensor'))
Inputs may be any that keep to these rules, and one draw needn't show every extreme that they name: `segment_ids`: segment numbers never fall along a replica's tokens; each segment holds 1 to 128 tokens.
All inputs are finite; a program needn't handle non-finite values.
Results may differ from a plain program's by a relative error of at most 0.023.
Values may be sent and summed in bfloat16 or wider, within the bound.
A program may use at most 128 MiB of HBM per device.

v0:
```python
import jax
import jax.numpy as jnp
from jax import lax
from jax.sharding import PartitionSpec as P

HD = 128


def layer_norm(values, gain):
    mean = jnp.mean(values, axis=-1, keepdims=True)
    second = jnp.mean(values * values, axis=-1, keepdims=True)
    return (values - mean) * lax.rsqrt(second - mean * mean + 1e-05) * gain


def per_device(
    tokens, segment_ids, gain_attn, w_query, w_key, w_value, w_output, gain_ffn, w_up, w_down
):
    tok_rows = tokens.shape[0]
    width = gain_attn.shape[0]
    groups = lax.axis_size(("section", "tensor"))
    share = width // groups
    first_col = lax.axis_index(("section", "tensor")) * share
    whole = lax.all_gather(tokens, ("section", "tensor"), axis=1, tiled=True)
    normed = layer_norm(whole.astype(jnp.float32), gain_attn).astype(jnp.bfloat16)
    local_heads = w_query.shape[1] // HD
    query = jnp.dot(normed, w_query, preferred_element_type=jnp.float32).astype(jnp.bfloat16)
    key = jnp.dot(normed, w_key, preferred_element_type=jnp.float32).astype(jnp.bfloat16)
    value = jnp.dot(normed, w_value, preferred_element_type=jnp.float32).astype(jnp.bfloat16)
    query = query.reshape(tok_rows, local_heads, HD)
    key = key.reshape(tok_rows, local_heads, HD)
    value = value.reshape(tok_rows, local_heads, HD)
    scores = jnp.einsum("qhd,khd->hqk", query, key, preferred_element_type=jnp.float32) * HD ** (
        -0.5
    )
    position = jnp.arange(tok_rows)
    segment_row = segment_ids[0]
    keep = jnp.logical_and(
        position[:, None] >= position[None, :], segment_row[:, None] == segment_row[None, :]
    )
    scores = jnp.where(keep[None], scores, -1e30)
    top = jnp.max(scores, axis=-1, keepdims=True)
    expo = jnp.exp(scores - top)
    probs = (expo / jnp.sum(expo, axis=-1, keepdims=True)).astype(jnp.bfloat16)
    context = jnp.einsum("hqk,khd->qhd", probs, value, preferred_element_type=jnp.float32)
    context = context.astype(jnp.bfloat16).reshape(tok_rows, local_heads * HD)
    partial_out = jnp.dot(context, w_output, preferred_element_type=jnp.float32)
    summed = lax.psum(partial_out.astype(jnp.bfloat16), ("section", "tensor")).astype(jnp.float32)
    resid_full = (whole.astype(jnp.float32) + summed).astype(jnp.bfloat16)
    normed_full = layer_norm(resid_full.astype(jnp.float32), gain_ffn).astype(jnp.bfloat16)
    normed_ffn = lax.dynamic_slice_in_dim(normed_full, first_col, share, 1)
    resid_mid = lax.dynamic_slice_in_dim(resid_full, first_col, share, 1)
    gathered = lax.all_gather(normed_ffn, "dp", axis=0, tiled=True)
    pre_act = lax.psum_scatter(
        jnp.dot(gathered, w_up, preferred_element_type=jnp.float32).astype(jnp.bfloat16),
        ("section", "tensor"),
        scatter_dimension=0,
        tiled=True,
    ).astype(jnp.float32)
    activated = jax.nn.gelu(pre_act, approximate=True).astype(jnp.bfloat16)
    partial_down = jnp.dot(
        lax.all_gather(activated, ("section", "tensor"), axis=0, tiled=True),
        w_down,
        preferred_element_type=jnp.float32,
    )
    ffn_out = lax.psum_scatter(
        partial_down.astype(jnp.bfloat16), "dp", scatter_dimension=0, tiled=True
    ).astype(jnp.float32)
    return (resid_mid.astype(jnp.float32) + ffn_out).astype(jnp.bfloat16)


def solution(mesh):
    return jax.shard_map(
        per_device,
        mesh=mesh,
        in_specs=(
            P("dp", ("section", "tensor")),
            P("dp", None),
            P(),
            P(None, ("section", "tensor")),
            P(None, ("section", "tensor")),
            P(None, ("section", "tensor")),
            P(("section", "tensor"), None),
            P(),
            P(("section", "tensor"), "dp"),
            P("dp", ("section", "tensor")),
        ),
        out_specs=P("dp", ("section", "tensor")),
        check_vma=False,
    )
```

profile of v0, /device:TPU:0, one launch (start us, length us, event | category | flops | bytes accessed | tf_op | source)
XLA Modules:
  0.0 492.6 jit_solution(8370720796275052697)
XLA Ops:
  6.5 0.7 all-gather.4.cloned.1.call-update
  7.3 0.9 fusion.18
  8.2 40.8 %all-gather.4.cloned.1.call-done = bf16[256,8192]{1,0:T(8,128)(2,1)} async-done(((bf16[256,512]{1,0:T(8,128)(2,1)}), bf16[256,8192]{1,0:T(8,128)(2,1)}) %all-gather.4.cloned.1.call-update) | async-done | bytes 4194320 | tf_op jit(solution)/shard_map/all_gather | solution.py:23
  49.0 3.5 convert_reduce_fusion
  52.5 1.8 fusion.3
  54.7 1.8 convolution_convert_fusion.4
  56.9 1.6 copy-done.6
  58.4 1.8 convolution_convert_fusion.5
  60.9 5.2 %convolution_convert_fusion.6 = bf16[256,256]{0,1:T(8,128)(2,1)S(1)} fusion(bf16[256,8192]{1,0:T(8,128)(2,1)} %copy-done.2, bf16[8192,256]{1,0:T(8,128)(2,1)} %param.15), kind=kOutput, calls=%fused_computation.26 | convolution fusion | flops 1073807360 | bytes 8519680 | tf_op jit(solution)/shard_map/dot_general | solution.py:28
  66.4 5.4 %convolution_convert_fusion = bf16[256,8192]{1,0:T(8,128)(2,1)} fusion(bf16[256,256]{0,1:T(8,128)(2,1)S(1)} %bitcast.30, bf16[256,8192]{1,0:T(8,128)(2,1)} %param.16), kind=kOutput, calls=%fused_computation.5 | convolution fusion | flops 1075838976 | bytes 8519680 | tf_op jit(solution)/shard_map/dot_general | solution.py:46
  72.1 0.8 dynamic-slice
  72.9 128.7 %all-reduce.2.cloned.1.call-done = bf16[256,8192]{1,0:T(8,128)(2,1)} async-done(((bf16[256,8192]{1,0:T(8,128)(2,1)}), bf16[256,8192]{1,0:T(8,128)(2,1)}) %all-reduce.2.cloned.1.call-update) | async-done | bytes 4194320 | tf_op jit(solution)/shard_map/psum | solution.py:47
  201.6 4.6 convert_reduce_fusion.1
  206.2 1.0 convert_element_type.73
  207.2 1.0 copy-done.4
  208.2 0.9 fusion.17
  209.1 54.6 %all-gather.6.cloned.1.call-done = bf16[2048,512]{1,0:T(8,128)(2,1)} async-done(((bf16[256,512]{1,0:T(8,128)(2,1)}), bf16[2048,512]{1,0:T(8,128)(2,1)}) %all-gather.6.cloned.1.call-update) | async-done | bytes 2097168 | tf_op jit(solution)/shard_map/all_gather | solution.py:52
  263.7 8.3 %convolution_convert_fusion.1 = bf16[2048,2048]{1,0:T(8,128)(2,1)} fusion(bf16[2048,512]{1,0:T(8,128)(2,1)} %all-gather.6.cloned.1.call-done, bf16[512,2048]{1,0:T(8,128)(2,1)S(1)} %copy-done), kind=kOutput, calls=%fused_computation.12 | convolution fusion | flops 4299161600 | bytes 12582912 | tf_op jit(solution)/shard_map/dot_general | solution.py:54
  272.1 73.0 %reduce-scatter.3.cloned.1.call-done = bf16[128,2048]{1,0:T(8,128)(2,1)} async-done(((bf16[2048,2048]{1,0:T(8,128)(2,1)}), bf16[128,2048]{1,0:T(8,128)(2,1)}) %reduce-scatter.3.cloned.1.call-update) | async-done | bytes 524304 | tf_op jit(solution)/shard_map/reduce_scatter | solution.py:53
  345.1 2.2 fusion.14
  347.5 50.4 %all-gather.8.cloned.1.call-done = bf16[2048,2048]{1,0:T(8,128)(2,1)} async-done(((bf16[128,2048]{1,0:T(8,128)(2,1)}), bf16[2048,2048]{1,0:T(8,128)(2,1)}) %all-gather.8.cloned.1.call-update) | async-done | bytes 8388624 | tf_op jit(solution)/shard_map/all_gather | solution.py:61
  397.9 10.0 %convolution_convert_fusion.2 = bf16[2048,512]{1,0:T(8,128)(2,1)} fusion(bf16[2048,2048]{1,0:T(8,128)(2,1)} %all-gather.8.cloned.1.call-done, bf16[2048,512]{1,0:T(8,128)(2,1)} %param.19), kind=kOutput, calls=%fused_computation.14 | convolution fusion | flops 4296015872 | bytes 12582912 | tf_op jit(solution)/shard_map/dot_general | solution.py:60
  407.9 76.0 %reduce-scatter.5.cloned.1.call-done = bf16[256,512]{1,0:T(8,128)(2,1)} async-done(((bf16[2048,512]{1,0:T(8,128)(2,1)}), bf16[256,512]{1,0:T(8,128)(2,1)}) %reduce-scatter.5.cloned.1.call-update) | async-done | bytes 262160 | tf_op jit(solution)/shard_map/reduce_scatter | solution.py:65
  484.0 1.8 add_convert_fusion
  (30 shorter events, 2.1 us)
Async XLA Ops:
  6.5 257.2 %copy-start = (bf16[512,2048]{1,0:T(8,128)(2,1)S(1)}, bf16[512,2048]{1,0:T(8,128)(2,1)}, u32[]{:S(2)}) copy-start(bf16[512,2048]{1,0:T(8,128)(2,1)} %param.18) | copy-start | bytes 6291460
  6.5 46.0 %copy-start.7 = (f32[8192]{0:T(1024)S(1)}, f32[8192]{0:T(1024)}, u32[]{:S(2)}) copy-start(f32[8192]{0:T(1024)} %param.12) | copy-start | bytes 98308
  6.5 42.4 %all-gather.4.cloned.1.call-start = ((), (), s32[]{:S(2)}) async-start(), calls=%async_computation.2 | async-start | bytes 4456448 | tf_op jit(solution)/shard_map/all_gather | solution.py:23
  7.3 194.3 %all-reduce.2.cloned.1.call-start = ((), (), s32[]{:S(2)}) async-start(), calls=%async_computation.3 | async-start | bytes 8388608 | tf_op jit(solution)/shard_map/psum | solution.py:47
  49.0 3.6 copy-start.3
  52.5 2.2 copy-start.5
  54.7 2.1 copy-start.2
  54.7 3.7 copy-start.6
  71.9 191.8 %all-gather.6.cloned.1.call-start = ((), (), s32[]{:S(2)}) async-start(), calls=%async_computation.4 | async-start | bytes 2359296 | tf_op jit(solution)/shard_map/all_gather | solution.py:52
  206.2 2.0 copy-start.4
  209.1 136.1 %reduce-scatter.3.cloned.1.call-start = ((), (), s32[]{:S(2)}) async-start(), calls=%async_computation.5 | async-start | bytes 8912896 | tf_op jit(solution)/shard_map/reduce_scatter | solution.py:53
  272.0 125.8 %all-gather.8.cloned.1.call-start = ((), (), s32[]{:S(2)}) async-start(), calls=%async_computation.6 | async-start | bytes 8912896 | tf_op jit(solution)/shard_map/all_gather | solution.py:61
  347.4 136.6 %reduce-scatter.5.cloned.1.call-start = ((), (), s32[]{:S(2)}) async-start(), calls=%async_computation.7 | async-start | bytes 2359296 | tf_op jit(solution)/shard_map/reduce_scatter | solution.py:65
  397.9 87.9 %copy-start.1 = (bf16[512,2048]{1,0:T(8,128)(2,1)S(1)}, bf16[512,2048]{1,0:T(8,128)(2,1)}, u32[]{:S(2)}) copy-start(bf16[512,2048]{1,0:T(8,128)(2,1)} %param.18) | copy-start | bytes 6291460
Sparse Core Ops, SparseCore 0:
  9.0 39.8 all-gather.3
  72.0 129.5 all-reduce.1
  209.2 54.4 all-gather.5
  272.2 72.9 reduce-scatter.2
  347.5 50.3 all-gather.7
  408.0 75.8 reduce-scatter.4
where the time goes:
time: 493 us
  waiting for transfers between devices  424 us (86%)
  matrix products  33.5 us (7%)
  other arithmetic  16.6 us (3%)
  between operations  13.6 us (3%)
    psum x1, waiting for transfers between devices, per_device(): lax.psum(partial_out.astype(jnp.bfloat16), ('section', 'tensor'))  129 us
    reduce_scatter x1, waiting for transfers between devices, per_device(): lax.psum_scatter(partial_down.astype(jnp.bfloat16), 'dp', scatter_dimensi...  76 us
    reduce_scatter x1, waiting for transfers between devices, per_device(): lax.psum_scatter(jnp.dot(gathered, w_up, preferred_element_type=jnp.float...  73 us
    all_gather x1, waiting for transfers between devices, per_device(): gathered = lax.all_gather(normed_ffn, 'dp', axis=0, tiled=True)  54.6 us
    all_gather x1, waiting for transfers between devices, per_device(): lax.all_gather(activated, ('section', 'tensor'), axis=0, tiled=True)  50.4 us
    all_gather x1, waiting for transfers between devices, per_device(): whole = lax.all_gather(tokens, ('section', 'tensor'), axis=1, tiled=True)  40.8 us
    dot_general x1, matrix products, per_device(): jnp.dot(lax.all_gather(activated, ('section', 'tensor'), axis=0, tiled=Tr...  9.99 us
  transfers between devices with their start and end apart: 6, of which 6 were waited for; matrix products, arithmetic and copies ran while one was open for 0% of the time, Pallas kernels for 0%

commit v1 on v0

--- a/solution.py
+++ b/solution.py
@@ -44,7 +44,9 @@
     context = jnp.einsum("hqk,khd->qhd", probs, value, preferred_element_type=jnp.float32)
     context = context.astype(jnp.bfloat16).reshape(tok_rows, local_heads * HD)
     partial_out = jnp.dot(context, w_output, preferred_element_type=jnp.float32)
-    summed = lax.psum(partial_out.astype(jnp.bfloat16), ("section", "tensor")).astype(jnp.float32)
+    summed = lax.psum(lax.psum(partial_out.astype(jnp.bfloat16), "tensor"), "section").astype(
+        jnp.float32
+    )
     resid_full = (whole.astype(jnp.float32) + summed).astype(jnp.bfloat16)
     normed_full = layer_norm(resid_full.astype(jnp.float32), gain_ffn).astype(jnp.bfloat16)
     normed_ffn = lax.dynamic_slice_in_dim(normed_full, first_col, share, 1)

time: 493 us -> 554 us (1.12)
  waiting for transfers between devices: 424 us -> 485 us
    psum x1 -> x2, waiting for transfers between devices: 129 us -> 189 us  [the longest x1 116 us: per_device(): lax.psum(lax.psum(partial_out.astype(jnp.bfloat16), 'tensor'), 'section')]
  transfers between devices with their start and end apart: 6 -> 7, of which waited for: 6 -> 7; matrix products, arithmetic and copies ran while one was open for 0% -> 0% of each run, Pallas kernels for 0% -> 0%
where the time goes in v1:
time: 554 us; the launch traced here: 553 us
  waiting for transfers between devices  485 us (88%)
  matrix products  33.5 us (6%)
  other arithmetic  16.6 us (3%)
  between operations  13.6 us (2%)
    psum x1, waiting for transfers between devices, per_device(): lax.psum(lax.psum(partial_out.astype(jnp.bfloat16), 'tensor'), 'section')  116 us
    reduce_scatter x1, waiting for transfers between devices, per_device(): lax.psum_scatter(partial_down.astype(jnp.bfloat16), 'dp', scatter_dimensi...  76.1 us
    reduce_scatter x1, waiting for transfers between devices, per_device(): lax.psum_scatter(jnp.dot(gathered, w_up, preferred_element_type=jnp.float...  73.1 us
    psum x1, waiting for transfers between devices, per_device(): lax.psum(partial_out.astype(jnp.bfloat16), 'tensor')  73 us
    all_gather x1, waiting for transfers between devices, per_device(): gathered = lax.all_gather(normed_ffn, 'dp', axis=0, tiled=True)  54.9 us
    all_gather x1, waiting for transfers between devices, per_device(): lax.all_gather(activated, ('section', 'tensor'), axis=0, tiled=True)  50.4 us
    all_gather x1, waiting for transfers between devices, per_device(): whole = lax.all_gather(tokens, ('section', 'tensor'), axis=1, tiled=True)  40.8 us
  transfers between devices with their start and end apart: 7, of which 7 were waited for; matrix products, arithmetic and copies ran while one was open for 0% of the time, Pallas kernels for 0%

profile of v1, /device:TPU:0, one launch (start us, length us, event | category | flops | bytes accessed | tf_op | source)
XLA Modules:
  0.0 553.3 jit_solution(15051552502903201443)
XLA Ops:
  7.3 0.9 fusion.18
  8.2 40.8 %all-gather.4.cloned.1.call-done = bf16[256,8192]{1,0:T(8,128)(2,1)} async-done(((bf16[256,512]{1,0:T(8,128)(2,1)}), bf16[256,8192]{1,0:T(8,128)(2,1)}) %all-gather.4.cloned.1.call-update) | async-done | bytes 4194320 | tf_op jit(solution)/shard_map/all_gather | solution.py:23
  49.0 3.5 convert_reduce_fusion
  52.5 1.8 fusion.3
  54.7 1.8 convolution_convert_fusion.4
  56.9 1.6 copy-done.6
  58.4 1.8 convolution_convert_fusion.5
  60.9 5.2 convolution_convert_fusion.6
  66.4 5.4 convolution_convert_fusion
  71.9 73.0 %all-reduce.3.cloned.1.call-done = bf16[256,8192]{1,0:T(8,128)(2,1)} async-done(((bf16[256,8192]{1,0:T(8,128)(2,1)}), bf16[256,8192]{1,0:T(8,128)(2,1)}) %all-reduce.3.cloned.1.call-update) | async-done | bytes 4194320 | tf_op jit(solution)/shard_map/psum | solution.py:47
  145.2 0.8 dynamic-slice
  146.0 115.9 %all-reduce.5.cloned.1.call-done = bf16[256,8192]{1,0:T(8,128)(2,1)} async-done(((bf16[256,8192]{1,0:T(8,128)(2,1)}), bf16[256,8192]{1,0:T(8,128)(2,1)}) %all-reduce.5.cloned.1.call-update) | async-done | bytes 4194320 | tf_op jit(solution)/shard_map/psum | solution.py:47
  261.9 4.6 convert_reduce_fusion.1
  266.5 1.0 convert_element_type.73
  267.5 1.0 copy-done.4
  268.5 0.9 fusion.17
  269.4 54.9 %all-gather.6.cloned.1.call-done = bf16[2048,512]{1,0:T(8,128)(2,1)} async-done(((bf16[256,512]{1,0:T(8,128)(2,1)}), bf16[2048,512]{1,0:T(8,128)(2,1)}) %all-gather.6.cloned.1.call-update) | async-done | bytes 2097168 | tf_op jit(solution)/shard_map/all_gather | solution.py:54
  324.4 8.3 %convolution_convert_fusion.1 = bf16[2048,2048]{1,0:T(8,128)(2,1)} fusion(bf16[2048,512]{1,0:T(8,128)(2,1)} %all-gather.6.cloned.1.call-done, bf16[512,2048]{1,0:T(8,128)(2,1)S(1)} %copy-done), kind=kOutput, calls=%fused_computation.12 | convolution fusion | flops 4299161600 | bytes 12582912 | tf_op jit(solution)/shard_map/dot_general | solution.py:56
  332.8 73.1 %reduce-scatter.3.cloned.1.call-done = bf16[128,2048]{1,0:T(8,128)(2,1)} async-done(((bf16[2048,2048]{1,0:T(8,128)(2,1)}), bf16[128,2048]{1,0:T(8,128)(2,1)}) %reduce-scatter.3.cloned.1.call-update) | async-done | bytes 524304 | tf_op jit(solution)/shard_map/reduce_scatter | solution.py:55
  405.9 2.2 fusion.14
  408.2 50.4 %all-gather.8.cloned.1.call-done = bf16[2048,2048]{1,0:T(8,128)(2,1)} async-done(((bf16[128,2048]{1,0:T(8,128)(2,1)}), bf16[2048,2048]{1,0:T(8,128)(2,1)}) %all-gather.8.cloned.1.call-update) | async-done | bytes 8388624 | tf_op jit(solution)/shard_map/all_gather | solution.py:63
  458.6 10.0 %convolution_convert_fusion.2 = bf16[2048,512]{1,0:T(8,128)(2,1)} fusion(bf16[2048,2048]{1,0:T(8,128)(2,1)} %all-gather.8.cloned.1.call-done, bf16[2048,512]{1,0:T(8,128)(2,1)} %param.19), kind=kOutput, calls=%fused_computation.14 | convolution fusion | flops 4296015872 | bytes 12582912 | tf_op jit(solution)/shard_map/dot_general | solution.py:62
  468.6 76.1 %reduce-scatter.5.cloned.1.call-done = bf16[256,512]{1,0:T(8,128)(2,1)} async-done(((bf16[2048,512]{1,0:T(8,128)(2,1)}), bf16[256,512]{1,0:T(8,128)(2,1)}) %reduce-scatter.5.cloned.1.call-update) | async-done | bytes 262160 | tf_op jit(solution)/shard_map/reduce_scatter | solution.py:67
  544.7 1.8 add_convert_fusion
  (33 shorter events, 2.9 us)
Async XLA Ops:
  6.5 317.9 %copy-start = (bf16[512,2048]{1,0:T(8,128)(2,1)S(1)}, bf16[512,2048]{1,0:T(8,128)(2,1)}, u32[]{:S(2)}) copy-start(bf16[512,2048]{1,0:T(8,128)(2,1)} %param.18) | copy-start | bytes 6291460
  6.5 46.0 %copy-start.7 = (f32[8192]{0:T(1024)S(1)}, f32[8192]{0:T(1024)}, u32[]{:S(2)}) copy-start(f32[8192]{0:T(1024)} %param.12) | copy-start | bytes 98308
  6.5 42.4 %all-gather.4.cloned.1.call-start = ((), (), s32[]{:S(2)}) async-start(), calls=%async_computation.2 | async-start | bytes 4456448 | tf_op jit(solution)/shard_map/all_gather | solution.py:23
  7.3 137.7 %all-reduce.3.cloned.1.call-start = ((), (), s32[]{:S(2)}) async-start(), calls=%async_computation.3 | async-start | bytes 8388608 | tf_op jit(solution)/shard_map/psum | solution.py:47
  49.0 3.6 copy-start.3
  52.5 2.2 copy-start.5
  54.7 2.1 copy-start.2
  54.7 3.7 copy-start.6
  71.9 190.0 %all-reduce.5.cloned.1.call-start = ((), (), s32[]{:S(2)}) async-start(), calls=%async_computation.4 | async-start | bytes 8388608 | tf_op jit(solution)/shard_map/psum | solution.py:47
  145.0 179.4 %all-gather.6.cloned.1.call-start = ((), (), s32[]{:S(2)}) async-start(), calls=%async_computation.5 | async-start | bytes 2359296 | tf_op jit(solution)/shard_map/all_gather | solution.py:54
  266.5 2.0 copy-start.4
  269.4 136.5 %reduce-scatter.3.cloned.1.call-start = ((), (), s32[]{:S(2)}) async-start(), calls=%async_computation.6 | async-start | bytes 8912896 | tf_op jit(solution)/shard_map/reduce_scatter | solution.py:55
  332.7 125.8 %all-gather.8.cloned.1.call-start = ((), (), s32[]{:S(2)}) async-start(), calls=%async_computation.7 | async-start | bytes 8912896 | tf_op jit(solution)/shard_map/all_gather | solution.py:63
  408.1 136.5 %reduce-scatter.5.cloned.1.call-start = ((), (), s32[]{:S(2)}) async-start(), calls=%async_computation.8 | async-start | bytes 2359296 | tf_op jit(solution)/shard_map/reduce_scatter | solution.py:67
  458.6 87.9 %copy-start.1 = (bf16[512,2048]{1,0:T(8,128)(2,1)S(1)}, bf16[512,2048]{1,0:T(8,128)(2,1)}, u32[]{:S(2)}) copy-start(bf16[512,2048]{1,0:T(8,128)(2,1)} %param.18) | copy-start | bytes 6291460
Sparse Core Ops, SparseCore 0:
  9.0 39.8 all-gather.3
  72.0 72.9 all-reduce.2
  147.6 114.3 all-reduce.4
  269.5 54.8 all-gather.5
  332.8 72.9 reduce-scatter.2
  408.2 50.2 all-gather.7
  468.7 75.8 reduce-scatter.4
